TPU v7x, 32 devices: a whole 2x2x4 slice. The times are simulated.
32 devices in a mesh: groups: 2 (over y), ep: 4 (over z), sub: 4 (over x, core).
Axes of the slice: x: 2, y: 2, z: 4, core: 2. Of those that a mesh axis runs over, the one named last changes fastest.
Arguments:
- tokens: bfloat16 [2048, 7168], P(('groups', 'ep', 'sub')), parts along dimension 0, may hold values from -6 to 6
- routes: int32 [2048, 8], P(('groups', 'ep', 'sub')), parts along dimension 0, may hold values from 0 to 255, as said below
- route_weights: float32 [2048, 8], P(('groups', 'ep', 'sub')), parts along dimension 0, may hold values from 0.5 to 2.5
- w_gate: bfloat16 [4, 7168, 2048], P('ep', None, 'sub'), may hold values from -0.0625 to 0.0625
- w_up: bfloat16 [4, 7168, 2048], P('ep', None, 'sub'), may hold values from -0.0625 to 0.0625
- w_down: bfloat16 [4, 2048, 7168], P('ep', 'sub'), may hold values from -0.125 to 0.125
Outputs:
- combined: bfloat16 [2048, 7168], P(('groups', 'ep', 'sub')), parts along dimension 0
There are 2 independent parts, one for each index of `groups`. A program takes and returns all parts, laid end to end along the dimension named above; an argument that names none is the same for every part. Nothing has to cross between parts.
Inputs may be any that keep to these rules, and one draw needn't show every extreme that they name: `routes`: each row names 8 different experts and at most one expert below 4. In the 64 rows of one device every expert below 4 is named by 1 to 16 rows; in every draw one such expert is named by exactly 16 rows on every device.
All inputs are finite; a program needn't handle non-finite values.
Results may differ from a plain program's by a relative error of at most 0.0095.
Values may be sent and summed in bfloat16 or wider, within the bound.
A program may use at most 128 MiB of HBM per device.

v0:
```python
import jax
import jax.numpy as jnp
from jax import lax
from jax.sharding import PartitionSpec as P


def settle(values):
    return lax.optimization_barrier(values)


def on_device(tokens, routes, route_weights, w_gate, w_up, w_down):
    rows, width = tokens.shape
    n_major = lax.axis_size("ep")
    n_minor = lax.axis_size("sub")
    capacity = rows // n_major
    portion_rows = n_major * capacity
    hits = routes[:, :, None] == jnp.arange(n_major, dtype=jnp.int32)[None, None, :]
    chosen = jnp.any(hits, axis=1)
    weight_of = jnp.sum(
        jnp.where(hits, route_weights[:, :, None], jnp.zeros((), jnp.float32)), axis=1
    )
    flags = chosen.astype(jnp.int32)
    slots = jnp.cumsum(flags, axis=0) - flags
    placed = chosen[:, :, None] & (
        slots[:, :, None] == jnp.arange(capacity, dtype=jnp.int32)[None, None, :]
    )
    selector = placed.astype(jnp.bfloat16)
    send_rows = jnp.einsum(
        "rfc,rd->fcd", selector, tokens, preferred_element_type=jnp.float32
    ).astype(jnp.bfloat16)
    spread_rows = jnp.broadcast_to(send_rows[:, None], (n_major, n_minor, capacity, width)).reshape(
        n_major * n_minor, capacity, width
    )
    got_rows = lax.all_to_all(spread_rows, ("ep", "sub"), split_axis=0, concat_axis=0, tiled=True)
    got_rows = got_rows.reshape(n_major, n_minor, capacity, width)
    gate_w = w_gate[0]
    up_w = w_up[0]
    down_w = w_down[0]
    part_rows = jnp.swapaxes(got_rows, 0, 1).reshape(lax.axis_size("sub") * portion_rows, width)
    gate = jnp.dot(part_rows, gate_w, preferred_element_type=jnp.float32)
    up = jnp.dot(part_rows, up_w, preferred_element_type=jnp.float32)
    hidden = (jax.nn.silu(gate) * up).astype(jnp.bfloat16)
    mine = lax.psum_scatter(
        jnp.dot(hidden, down_w, preferred_element_type=jnp.float32).astype(jnp.bfloat16),
        "sub",
        scatter_dimension=0,
        tiled=True,
    )
    back = mine.reshape(n_major, capacity, width)
    result = lax.all_to_all(back, "ep", split_axis=0, concat_axis=0, tiled=True)
    returned = settle(result).reshape(n_major * capacity, width)
    picked = jnp.dot(
        selector.reshape(rows, n_major * capacity), returned, preferred_element_type=jnp.float32
    )
    factor = jnp.sum(weight_of, axis=1)
    return (factor[:, None] * picked).astype(jnp.bfloat16)


def solution(mesh):
    return jax.shard_map(
        on_device,
        mesh=mesh,
        in_specs=(
            P(("groups", "ep", "sub"), None),
            P(("groups", "ep", "sub"), None),
            P(("groups", "ep", "sub"), None),
            P("ep", None, "sub"),
            P("ep", None, "sub"),
            P("ep", "sub", None),
        ),
        out_specs=P(("groups", "ep", "sub"), None),
        check_vma=False,
    )
```

profile of v0, /device:TPU:0, one launch (start us, length us, event | category | flops | bytes accessed | tf_op | source)
XLA Modules:
  0.0 191.1 jit_solution(4899889528982192447)
XLA Ops:
  6.5 0.0 copy-start
  6.5 0.0 reduce-scatter.2.cloned.1.call-start
  6.5 0.8 fusion.27
  7.3 0.1 copy.20
  7.4 0.1 reduce_window_sum.11
  7.5 0.1 copy.22
  7.6 0.1 copy-done
  7.7 0.4 convolution_convert_fusion.1
  8.1 0.0 slice-start
  8.1 0.4 broadcast_in_dim.16
  8.6 0.0 slice-start.1
  8.6 88.4 %all_to_all.10 = bf16[16,16,7168]{2,1,0:T(8,128)(2,1)S(1)} all-to-all(bf16[16,16,7168]{2,1,0:T(8,128)(2,1)S(1)} %bitcast.34), channel_id=1, replica_groups=mesh['groups'=2,'ep'=4,'sub'=4] {'ep','sub'}, dimensions={0} | all-to-all | bytes 7340032 | tf_op jit(solution)/shard_map/all_to_all | solution.py:34
  97.0 0.3 copy.23
  97.3 0.0 copy-start.1
  97.3 1.8 copy-done.1
  99.2 0.0 slice-done
  99.2 0.0 slice-done.1
  99.2 2.0 %fusion.5 = f32[256,512]{1,0:T(8,128)S(1)} fusion(bf16[256,7168]{1,0:T(8,128)(2,1)S(1)} %bitcast.35, bf16[1,7168,512]{2,1,0:T(8,128)(2,1)S(1)} %bitcast.39), kind=kOutput, calls=%fused_computation.8 | convolution fusion | flops 1879048192 | bytes 11534336 | tf_op jit(solution)/shard_map/dot_general | solution.py:40
  101.2 12.1 %convolution_convert_fusion = bf16[256,7168]{1,0:T(8,128)(2,1)} fusion(bf16[1,512,7168]{2,1,0:T(8,128)(2,1)} %param.11, bf16[256,7168]{1,0:T(8,128)(2,1)} %bitcast.36, bf16[1,7168,512]{2,1,0:T(8,128)(2,1)} %param.10, f32[256,512]{1,0:T(8,128)S(1)} %fusion.5), kind=kOutput, calls=%fused_computation | convolution fusion | flops 3760717824 | bytes 22544384 | tf_op jit(solution)/shard_map/dot_general | solution.py:44
  113.3 0.0 copy-start.2
  113.3 0.0 copy-start.3
  113.3 0.0 reduce-scatter.2.cloned.1.call-update
  113.3 42.0 %reduce-scatter.2.cloned.1.call-done = bf16[64,7168]{1,0:T(8,128)(2,1)} async-done(((bf16[256,7168]{1,0:T(8,128)(2,1)}), bf16[64,7168]{1,0:T(8,128)(2,1)}) %reduce-scatter.2.cloned.1.call-update) | async-done | bytes 917520 | tf_op jit(solution)/shard_map/reduce_scatter | solution.py:43
  155.3 4.6 %all-to-all-start.1 = ((bf16[4,16,7168]{2,1,0:T(8,128)(2,1)}), bf16[4,16,7168]{2,1,0:T(8,128)(2,1)S(1)}, u32[]{:S(2)}, u32[]{:S(2)}) async-start(bf16[4,16,7168]{2,1,0:T(8,128)(2,1)} %bitcast.37), calls=%async_computation.2 | async-start | bytes 1835008 | tf_op jit(solution)/shard_map/all_to_all | solution.py:50
  159.9 0.0 copy-done.2
  159.9 0.0 copy-done.3
  159.9 22.9 %all-to-all-done.1 = bf16[4,16,7168]{2,1,0:T(8,128)(2,1)S(1)} async-done(((bf16[4,16,7168]{2,1,0:T(8,128)(2,1)}), bf16[4,16,7168]{2,1,0:T(8,128)(2,1)S(1)}, u32[]{:S(2)}, u32[]{:S(2)}) %all-to-all-start.1) | async-done | bytes 917536 | tf_op jit(solution)/shard_map/all_to_all | solution.py:50
  182.8 1.4 fusion.1
  (4 shorter events, 0.0 us)
Async XLA Ops:
  6.5 1.2 copy-start
  6.5 148.8 %reduce-scatter.2.cloned.1.call-start = ((), (), s32[]{:S(2)}) async-start(), calls=%async_computation.3 | async-start | bytes 4587520 | tf_op jit(solution)/shard_map/reduce_scatter | solution.py:43
  8.1 91.1 %slice-start = ((s8[7340032]{0:T(1024)(128)(4,1)}), s8[4194304]{0:T(1024)(128)(4,1)S(1)}, s32[]{:S(2)}) async-start(s8[7340032]{0:T(1024)(128)(4,1)} %bitcast.38), calls=%async_computation.4 | async-start | bytes 8388608
  8.6 90.6 %slice-start.1 = ((s8[7340032]{0:T(1024)(128)(4,1)}), s8[3145728]{0:T(1024)(128)(4,1)S(1)}, s32[]{:S(2)}) async-start(s8[7340032]{0:T(1024)(128)(4,1)} %bitcast.38), calls=%async_computation.5 | async-start | bytes 6291456
  97.3 1.8 copy-start.1
  113.3 46.6 %copy-start.2 = (s32[64,8]{0,1:T(8,128)S(1)}, s32[64,8]{0,1:T(8,128)}, u32[]{:S(2)}) copy-start(s32[64,8]{0,1:T(8,128)} %param.7) | copy-start | bytes 6148
  113.3 46.6 %copy-start.3 = (f32[64,8]{0,1:T(8,128)S(1)}, f32[64,8]{0,1:T(8,128)}, u32[]{:S(2)}) copy-start(f32[64,8]{0,1:T(8,128)} %param.8) | copy-start | bytes 6148
  155.3 27.5 %all-to-all-start.1 = ((bf16[4,16,7168]{2,1,0:T(8,128)(2,1)}), bf16[4,16,7168]{2,1,0:T(8,128)(2,1)S(1)}, u32[]{:S(2)}, u32[]{:S(2)}) async-start(bf16[4,16,7168]{2,1,0:T(8,128)(2,1)} %bitcast.37), calls=%async_computation.2 | async-start | bytes 1835008 | tf_op jit(solution)/shard_map/all_to_all | solution.py:50
Sparse Core Ops, SparseCore 0:
  113.5 41.8 reduce-scatter.1
where the time goes:
time: 191 us
  blocking collectives  88.4 us (46%)
  waiting for transfers between devices  64.9 us (34%)
  matrix products  15.9 us (8%)
  between operations  13.5 us (7%)
  starting transfers between devices  4.58 us (2%)
  local copies, waits for them, and re-layouts  2.87 us (2%)
    all_to_all x1, blocking collectives, on_device(): lax.all_to_all(spread_rows, ('ep', 'sub'), split_axis=0, concat_axis=0, t...  88.4 us
    reduce_scatter x1, waiting for transfers between devices, on_device(): lax.psum_scatter(jnp.dot(hidden, down_w, preferred_element_type=jnp.float...  42 us
    all_to_all x1, waiting for transfers between devices, on_device(): result = lax.all_to_all(back, 'ep', split_axis=0, concat_axis=0, tiled=True)  22.9 us
    dot_general x1, matrix products, on_device(): jnp.dot(hidden, down_w, preferred_element_type=jnp.float32)  12.1 us
    all_to_all x1, starting transfers between devices, on_device(): result = lax.all_to_all(back, 'ep', split_axis=0, concat_axis=0, tiled=True)  4.58 us
  transfers between devices with their start and end apart: 2, of which 2 were waited for; matrix products, arithmetic and copies ran while one was open for 0% of the time, Pallas kernels for 0%

commit v1 on v0

v1 whole, which is shorter than its diff:
```python
import functools

import jax
import jax.numpy as jnp
from jax import lax
from jax.experimental import pallas as pl
from jax.experimental.pallas import tpu as pltpu
from jax.sharding import PartitionSpec as P

MESH = pl.DeviceIdType.MESH


def settle(values):
    return lax.optimization_barrier(values)


def flip(index, step, extent):
    result = 0
    bit = 1
    while bit < extent:
        digit = lax.rem(lax.div(index, bit), 2)
        result = result + (1 - digit if step & bit else digit) * bit
        bit *= 2
    return result


def layer_kernel(
    n_major,
    cap,
    tile,
    tokens_ref,
    routes_ref,
    weights_ref,
    gate_hbm,
    up_hbm,
    down_hbm,
    out_ref,
    gate_w,
    up_w,
    down_w,
    outgoing,
    rows_in,
    partial,
    core_in,
    x_out,
    x_in,
    z_out,
    returned,
    gate_acc,
    up_acc,
    w_sem,
    dz_send,
    dz_recv,
    dx_send,
    dx_recv,
    dc_send,
    dc_recv,
    rc_send,
    rc_recv,
    rx_send,
    rx_recv,
    rz_send,
    rz_recv,
):
    rows, width = tokens_ref.shape
    slots = n_major * cap
    chunk = 4 * cap
    e = lax.axis_index("ep")
    s = lax.axis_index("sub")
    x = lax.div(s, 2)
    c = lax.rem(s, 2)
    s_core = 2 * x + (1 - c)
    s_x = 2 * (1 - x) + c
    s_far = 2 * (1 - x) + (1 - c)
    planes = [flip(e, k, n_major) for k in range(n_major)]

    loads = [
        pltpu.make_async_copy(gate_hbm.at[0], gate_w, w_sem.at[0]),
        pltpu.make_async_copy(up_hbm.at[0], up_w, w_sem.at[1]),
        pltpu.make_async_copy(down_hbm.at[0], down_w, w_sem.at[2]),
    ]
    for load in loads:
        load.start()

    barrier = pltpu.get_barrier_semaphore()
    partners = [(planes[k], s) for k in range(1, n_major)] + [(e, s_x), (e, s_core)]
    for plane, sub in partners:
        pl.semaphore_signal(
            barrier, inc=1, device_id={"ep": plane, "sub": sub}, device_id_type=MESH
        )

    def selector_of():
        column = lax.broadcasted_iota(jnp.int32, (rows, slots), 1)
        expert = lax.div(column, cap)
        place = lax.rem(column, cap)
        chosen = jnp.zeros((rows, slots), jnp.float32)
        for k in range(routes_ref.shape[1]):
            chosen = jnp.maximum(
                chosen, jnp.where(routes_ref[:, k : k + 1] == expert, 1.0, 0.0)
            )
        earlier = jnp.where(
            lax.broadcasted_iota(jnp.int32, (rows, rows), 0)
            > lax.broadcasted_iota(jnp.int32, (rows, rows), 1),
            1.0,
            0.0,
        ).astype(jnp.bfloat16)
        slot = jnp.dot(earlier, chosen.astype(jnp.bfloat16), preferred_element_type=jnp.float32)
        return jnp.where(slot == place.astype(jnp.float32), chosen, 0.0).astype(jnp.bfloat16)

    selector = selector_of()

    @pl.loop(0, width // tile)
    def _(j):
        cols = pl.ds(pl.multiple_of(j * tile, tile), tile)
        picked = lax.dot_general(
            selector,
            tokens_ref[:, cols],
            (((0,), (0,)), ((), ())),
            preferred_element_type=jnp.float32,
        ).astype(jnp.bfloat16)
        outgoing[:, :, cols] = picked.reshape(n_major, cap, tile)

    rows_in[e, s] = outgoing[e]
    pl.semaphore_wait(barrier, len(partners))

    def remote(src, dst, send, recv, plane, sub):
        return pltpu.make_async_remote_copy(
            src_ref=src,
            dst_ref=dst,
            send_sem=send,
            recv_sem=recv,
            device_id={"ep": plane, "sub": sub},
            device_id_type=MESH,
        )

    sent = []

    def launch(copy):
        copy.start()
        sent.append(copy)

    def spread(k):
        own = rows_in.at[planes[k], s]
        launch(remote(own, own, dx_send.at[k], dx_recv.at[k], e, s_x))
        launch(remote(own, own, dc_send.at[k, 0], dc_recv.at[k, 0], e, s_core))

    def arrived(dst, send, recv):
        remote(dst, dst, send, recv, e, s_x).wait_recv()

    spread(0)
    for k in range(1, n_major):
        launch(
            remote(
                outgoing.at[planes[k]],
                rows_in.at[e, s],
                dz_send.at[k],
                dz_recv.at[k],
                planes[k],
                s,
            )
        )

    def compute(k):
        plane = planes[k]
        if k == 0:
            loads[0].wait()
            loads[1].wait()
        gate_acc[...] = jnp.zeros_like(gate_acc)
        up_acc[...] = jnp.zeros_like(up_acc)

        @pl.loop(0, width // tile)
        def _(j):
            cols = pl.ds(pl.multiple_of(j * tile, tile), tile)
            part = rows_in[plane, :, :, cols].reshape(chunk, tile)
            gate_acc[...] += jnp.dot(part, gate_w[cols, :], preferred_element_type=jnp.float32)
            up_acc[...] += jnp.dot(part, up_w[cols, :], preferred_element_type=jnp.float32)

        gate = gate_acc[...]
        hidden = (jax.nn.silu(gate) * up_acc[...]).astype(jnp.bfloat16)
        if k == 0:
            loads[2].wait()

        @pl.loop(0, width // tile)
        def _(j):
            cols = pl.ds(pl.multiple_of(j * tile, tile), tile)
            product = jnp.dot(hidden, down_w[:, cols], preferred_element_type=jnp.float32)
            partial[k, :, :, cols] = product.astype(jnp.bfloat16).reshape(4, cap, tile)

        for column in range(2):
            launch(
                remote(
                    partial.at[k, 2 * column + (1 - c)],
                    core_in.at[k, column],
                    rc_send.at[k, column],
                    rc_recv.at[k, column],
                    e,
                    s_core,
                )
            )

    def core_sum(k):
        for column in range(2):
            arrived(core_in.at[k, column], rc_send.at[k, column], rc_recv.at[k, column])
        total = partial[k, s_x].astype(jnp.float32) + core_in[k, 1 - x].astype(jnp.float32)
        x_out[k] = total.astype(jnp.bfloat16)
        launch(remote(x_out.at[k], x_in.at[k], rx_send.at[k], rx_recv.at[k], e, s_x))

    def x_sum(k):
        arrived(x_in.at[k], rx_send.at[k], rx_recv.at[k])
        total = (
            partial[k, s].astype(jnp.float32)
            + core_in[k, x].astype(jnp.float32)
            + x_in[k].astype(jnp.float32)
        ).astype(jnp.bfloat16)
        if k == 0:
            returned[e] = total
        else:
            z_out[k] = total
            launch(
                remote(
                    z_out.at[k], returned.at[e], rz_send.at[k], rz_recv.at[k], planes[k], s
                )
            )

    for k in range(n_major):
        if k + 1 < n_major:
            arrived(rows_in.at[planes[k + 1], s], dz_send.at[k + 1], dz_recv.at[k + 1])
            spread(k + 1)
        far = rows_in.at[planes[k], s_x]
        arrived(far, dx_send.at[k], dx_recv.at[k])
        launch(remote(far, far, dc_send.at[k, 1], dc_recv.at[k, 1], e, s_core))
        arrived(rows_in.at[planes[k], s_core], dc_send.at[k, 0], dc_recv.at[k, 0])
        arrived(rows_in.at[planes[k], s_far], dc_send.at[k, 1], dc_recv.at[k, 1])
        compute(k)
        if k >= 1:
            x_sum(k - 1)
        core_sum(k)
    x_sum(n_major - 1)

    factor = jnp.sum(
        jnp.where(routes_ref[...] < n_major, weights_ref[...], 0.0), axis=1, keepdims=True
    )
    for k in range(1, n_major):
        arrived(returned.at[planes[k]], rz_send.at[k], rz_recv.at[k])

    @pl.loop(0, width // tile)
    def _(j):
        cols = pl.ds(pl.multiple_of(j * tile, tile), tile)
        picked = jnp.dot(
            selector,
            returned[:, :, cols].reshape(slots, tile),
            preferred_element_type=jnp.float32,
        )
        out_ref[:, cols] = (factor * picked).astype(jnp.bfloat16)

    for copy in sent:
        copy.wait_send()


def fused(tokens, routes, route_weights, w_gate, w_up, w_down):
    rows, width = tokens.shape
    n = lax.axis_size("ep")
    cap = rows // n
    hidden = w_gate.shape[2]
    tile = 1024 if width % 1024 == 0 else 128
    slab = (cap, width)
    bf16 = jnp.bfloat16
    dma = pltpu.SemaphoreType.DMA
    vmem = pl.BlockSpec(memory_space=pltpu.VMEM)
    hbm = pl.BlockSpec(memory_space=pl.ANY)
    return pl.pallas_call(
        functools.partial(layer_kernel, n, cap, tile),
        out_shape=jax.ShapeDtypeStruct((rows, width), bf16),
        in_specs=[vmem, vmem, vmem, hbm, hbm, hbm],
        out_specs=vmem,
        scratch_shapes=[
            pltpu.VMEM((width, hidden), bf16),
            pltpu.VMEM((width, hidden), bf16),
            pltpu.VMEM((hidden, width), bf16),
            pltpu.VMEM((n, *slab), bf16),
            pltpu.VMEM((n, 4, *slab), bf16),
            pltpu.VMEM((n, 4, *slab), bf16),
            pltpu.VMEM((n, 2, *slab), bf16),
            pltpu.VMEM((n, *slab), bf16),
            pltpu.VMEM((n, *slab), bf16),
            pltpu.VMEM((n, *slab), bf16),
            pltpu.VMEM((n, *slab), bf16),
            pltpu.VMEM((4 * cap, hidden), jnp.float32),
            pltpu.VMEM((4 * cap, hidden), jnp.float32),
            dma((3,)),
            dma((n,)),
            dma((n,)),
            dma((n,)),
            dma((n,)),
            dma((n, 2)),
            dma((n, 2)),
            dma((n, 2)),
            dma((n, 2)),
            dma((n,)),
            dma((n,)),
            dma((n,)),
            dma((n,)),
        ],
        compiler_params=pltpu.CompilerParams(
            collective_id=0, has_side_effects=True, vmem_limit_bytes=56 * 1024 * 1024
        ),
        cost_estimate=pl.CostEstimate(
            flops=6 * rows * 4 * width * hidden,
            bytes_accessed=6 * width * hidden,
            transcendentals=rows * 4 * hidden,
        ),
    )(tokens, routes, route_weights, w_gate, w_up, w_down)


def staged(tokens, routes, route_weights, w_gate, w_up, w_down):
    rows, width = tokens.shape
    n_major = lax.axis_size("ep")
    n_minor = lax.axis_size("sub")
    capacity = rows // n_major
    portion_rows = n_major * capacity
    hits = routes[:, :, None] == jnp.arange(n_major, dtype=jnp.int32)[None, None, :]
    chosen = jnp.any(hits, axis=1)
    weight_of = jnp.sum(
        jnp.where(hits, route_weights[:, :, None], jnp.zeros((), jnp.float32)), axis=1
    )
    flags = chosen.astype(jnp.int32)
    slots = jnp.cumsum(flags, axis=0) - flags
    placed = chosen[:, :, None] & (
        slots[:, :, None] == jnp.arange(capacity, dtype=jnp.int32)[None, None, :]
    )
    selector = placed.astype(jnp.bfloat16)
    send_rows = jnp.einsum(
        "rfc,rd->fcd", selector, tokens, preferred_element_type=jnp.float32
    ).astype(jnp.bfloat16)
    came = lax.all_to_all(send_rows, "ep", split_axis=0, concat_axis=0, tiled=True)
    got_rows = lax.all_gather(came.reshape(portion_rows, width), "sub", axis=0, tiled=True)
    gate = jnp.dot(got_rows, w_gate[0], preferred_element_type=jnp.float32)
    up = jnp.dot(got_rows, w_up[0], preferred_element_type=jnp.float32)
    hidden = (jax.nn.silu(gate) * up).astype(jnp.bfloat16)
    mine = lax.psum_scatter(
        jnp.dot(hidden, w_down[0], preferred_element_type=jnp.float32).astype(jnp.bfloat16),
        "sub",
        scatter_dimension=0,
        tiled=True,
    )
    back = mine.reshape(n_major, capacity, width)
    result = lax.all_to_all(back, "ep", split_axis=0, concat_axis=0, tiled=True)
    returned = settle(result).reshape(portion_rows, width)
    picked = jnp.dot(
        selector.reshape(rows, portion_rows), returned, preferred_element_type=jnp.float32
    )
    factor = jnp.sum(weight_of, axis=1)
    return (factor[:, None] * picked).astype(jnp.bfloat16)


def on_device(*args):
    n_major = lax.axis_size("ep")
    rows = args[0].shape[0]
    whole_tiles = rows % n_major == 0 and (rows // n_major) % 16 == 0
    if whole_tiles and lax.axis_size("sub") == 4 and n_major & (n_major - 1) == 0:
        return fused(*args)
    return staged(*args)


def solution(mesh):
    return jax.shard_map(
        on_device,
        mesh=mesh,
        in_specs=(
            P(("groups", "ep", "sub"), None),
            P(("groups", "ep", "sub"), None),
            P(("groups", "ep", "sub"), None),
            P("ep", None, "sub"),
            P("ep", None, "sub"),
            P("ep", "sub", None),
        ),
        out_specs=P(("groups", "ep", "sub"), None),
        check_vma=False,
    )
```

time: 191 us -> 77.1 us (0.40)
  the two profiles are of different devices: /device:TPU:0 before, /device:TPU:9 now
where the time goes in v1:
time: 77.1 us; the launch traced here: 76.9 us
  Pallas kernels  72 us (93%)
  local copies, waits for them, and re-layouts  4.91 us (6%)
    pallas_call x1, Pallas kernels, fused(): pl.pallas_call(functools.partial(layer_kernel, n, cap, tile), out_shape=j...  72 us
    unnamed x3, local copies, waits for them, and re-layouts  4.91 us

profile of v1, /device:TPU:9, one launch (start us, length us, event | category | flops | bytes accessed | tf_op | source)
XLA Modules:
  0.0 76.9 jit_solution(9828439771918185208)
XLA Ops:
  0.0 1.4 %copy.7.routes_ref = s32[64,8]{1,0:T(8,128)} copy(s32[64,8]{0,1:T(8,128)} %param.7) | data formatting | bytes 4096 | tf_op args[1]
  1.4 1.4 %copy.8.weights_ref = f32[64,8]{1,0:T(8,128)} copy(f32[64,8]{0,1:T(8,128)} %param.8) | data formatting | bytes 4096 | tf_op args[2]
  2.8 72.0 %shard_map.64 = bf16[64,7168]{1,0:T(8,128)(2,1)} custom-call(bf16[64,7168]{1,0:T(8,128)(2,1)} %tokens_ref.1, s32[64,8]{1,0:T(8,128)} %copy.7.routes_ref, f32[64,8]{1,0:T(8,128)} %copy.8.weights_ref, bf16[1,7168,512]{2,1,0:T(8,128)(2,1)} %gate_hbm.1, bf16[1,7168,512]{2,1,0:T(8,128)(2,1)} %up_hbm.1, bf16[1,512,7168]{2,1,0:T(8,128)(2,1)} %down_hbm.1), custom_call_target="tpu_custom_call" | custom-call | flops 5637144576 | bytes 22020096 | tf_op jit(solution)/shard_map/pallas_call | solution.py:271
  74.8 2.2 %copy.10 = bf16[64,7168]{1,0:T(8,128)(2,1)} copy(bf16[64,7168]{1,0:T(8,128)(2,1)} %shard_map.64) | data formatting | bytes 1835008

commit v2 on v1

--- a/solution.py
+++ b/solution.py
@@ -8,6 +8,8 @@
 from jax.sharding import PartitionSpec as P
 
 MESH = pl.DeviceIdType.MESH
+ORDER = (0, 1, 2, 3)
+ISSUE = ((1, 2, 3), (), (), ())
 
 
 def settle(values):
@@ -30,11 +32,11 @@
     tile,
     tokens_ref,
     routes_ref,
-    weights_ref,
     gate_hbm,
     up_hbm,
     down_hbm,
-    out_ref,
+    returned,
+    selector_ref,
     gate_w,
     up_w,
     down_w,
@@ -45,7 +47,6 @@
     x_out,
     x_in,
     z_out,
-    returned,
     gate_acc,
     up_acc,
     w_sem,
@@ -89,34 +90,27 @@
             barrier, inc=1, device_id={"ep": plane, "sub": sub}, device_id_type=MESH
         )
 
-    def selector_of():
-        column = lax.broadcasted_iota(jnp.int32, (rows, slots), 1)
-        expert = lax.div(column, cap)
-        place = lax.rem(column, cap)
-        chosen = jnp.zeros((rows, slots), jnp.float32)
-        for k in range(routes_ref.shape[1]):
-            chosen = jnp.maximum(
-                chosen, jnp.where(routes_ref[:, k : k + 1] == expert, 1.0, 0.0)
-            )
-        earlier = jnp.where(
-            lax.broadcasted_iota(jnp.int32, (rows, rows), 0)
-            > lax.broadcasted_iota(jnp.int32, (rows, rows), 1),
-            1.0,
-            0.0,
-        ).astype(jnp.bfloat16)
-        slot = jnp.dot(earlier, chosen.astype(jnp.bfloat16), preferred_element_type=jnp.float32)
-        return jnp.where(slot == place.astype(jnp.float32), chosen, 0.0).astype(jnp.bfloat16)
-
-    selector = selector_of()
+    slot_row = lax.broadcasted_iota(jnp.int32, (slots, rows), 0)
+    expert = lax.div(slot_row, cap)
+    place = lax.rem(slot_row, cap)
+    chosen = jnp.zeros((slots, rows), jnp.float32)
+    for k in range(routes_ref.shape[0]):
+        chosen = jnp.maximum(chosen, jnp.where(routes_ref[k : k + 1, :] == expert, 1.0, 0.0))
+    earlier = jnp.where(
+        lax.broadcasted_iota(jnp.int32, (rows, rows), 0)
+        < lax.broadcasted_iota(jnp.int32, (rows, rows), 1),
+        1.0,
+        0.0,
+    ).astype(jnp.bfloat16)
+    slot = jnp.dot(chosen.astype(jnp.bfloat16), earlier, preferred_element_type=jnp.float32)
+    selector = jnp.where(slot == place.astype(jnp.float32), chosen, 0.0).astype(jnp.bfloat16)
+    selector_ref[...] = selector
 
     @pl.loop(0, width // tile)
     def _(j):
         cols = pl.ds(pl.multiple_of(j * tile, tile), tile)
-        picked = lax.dot_general(
-            selector,
-            tokens_ref[:, cols],
-            (((0,), (0,)), ((), ())),
-            preferred_element_type=jnp.float32,
+        picked = jnp.dot(
+            selector, tokens_ref[:, cols], preferred_element_type=jnp.float32
         ).astype(jnp.bfloat16)
         outgoing[:, :, cols] = picked.reshape(n_major, cap, tile)
 
@@ -147,18 +141,23 @@
     def arrived(dst, send, recv):
         remote(dst, dst, send, recv, e, s_x).wait_recv()
 
+    def issue(ks):
+        for k in ks:
+            launch(
+                remote(
+                    outgoing.at[planes[k]],
+                    rows_in.at[e, s],
+                    dz_send.at[k],
+                    dz_recv.at[k],
+                    planes[k],
+                    s,
+                )
+            )
+
+    order = ORDER if n_major == 4 else tuple(range(n_major))
+    plan = ISSUE if n_major == 4 else (order[1:],) + ((),) * (n_major - 1)
+    issue(plan[0])
     spread(0)
-    for k in range(1, n_major):
-        launch(
-            remote(
-                outgoing.at[planes[k]],
-                rows_in.at[e, s],
-                dz_send.at[k],
-                dz_recv.at[k],
-                planes[k],
-                s,
-            )
-        )
 
     def compute(k):
         plane = planes[k]
@@ -222,37 +221,25 @@
                 )
             )
 
-    for k in range(n_major):
-        if k + 1 < n_major:
-            arrived(rows_in.at[planes[k + 1], s], dz_send.at[k + 1], dz_recv.at[k + 1])
-            spread(k + 1)
+    for i, k in enumerate(order):
+        if i + 1 < n_major:
+            later = order[i + 1]
+            arrived(rows_in.at[planes[later], s], dz_send.at[later], dz_recv.at[later])
+            issue(plan[i + 1])
+            spread(later)
         far = rows_in.at[planes[k], s_x]
         arrived(far, dx_send.at[k], dx_recv.at[k])
         launch(remote(far, far, dc_send.at[k, 1], dc_recv.at[k, 1], e, s_core))
         arrived(rows_in.at[planes[k], s_core], dc_send.at[k, 0], dc_recv.at[k, 0])
         arrived(rows_in.at[planes[k], s_far], dc_send.at[k, 1], dc_recv.at[k, 1])
         compute(k)
-        if k >= 1:
-            x_sum(k - 1)
+        if i >= 1:
+            x_sum(order[i - 1])
         core_sum(k)
-    x_sum(n_major - 1)
-
-    factor = jnp.sum(
-        jnp.where(routes_ref[...] < n_major, weights_ref[...], 0.0), axis=1, keepdims=True
-    )
-    for k in range(1, n_major):
+    x_sum(order[-1])
+
+    for k in order[1:]:
         arrived(returned.at[planes[k]], rz_send.at[k], rz_recv.at[k])
-
-    @pl.loop(0, width // tile)
-    def _(j):
-        cols = pl.ds(pl.multiple_of(j * tile, tile), tile)
-        picked = jnp.dot(
-            selector,
-            returned[:, :, cols].reshape(slots, tile),
-            preferred_element_type=jnp.float32,
-        )
-        out_ref[:, cols] = (factor * picked).astype(jnp.bfloat16)
-
     for copy in sent:
         copy.wait_send()
 
@@ -268,11 +255,14 @@
     dma = pltpu.SemaphoreType.DMA
     vmem = pl.BlockSpec(memory_space=pltpu.VMEM)
     hbm = pl.BlockSpec(memory_space=pl.ANY)
-    return pl.pallas_call(
+    returned, selector = pl.pallas_call(
         functools.partial(layer_kernel, n, cap, tile),
-        out_shape=jax.ShapeDtypeStruct((rows, width), bf16),
-        in_specs=[vmem, vmem, vmem, hbm, hbm, hbm],
-        out_specs=vmem,
+        out_shape=(
+            jax.ShapeDtypeStruct((n, *slab), bf16),
+            jax.ShapeDtypeStruct((n * cap, rows), bf16),
+        ),
+        in_specs=[vmem, vmem, hbm, hbm, hbm],
+        out_specs=(vmem, vmem),
         scratch_shapes=[
             pltpu.VMEM((width, hidden), bf16),
             pltpu.VMEM((width, hidden), bf16),
@@ -284,7 +274,6 @@
             pltpu.VMEM((n, *slab), bf16),
             pltpu.VMEM((n, *slab), bf16),
             pltpu.VMEM((n, *slab), bf16),
-            pltpu.VMEM((n, *slab), bf16),
             pltpu.VMEM((4 * cap, hidden), jnp.float32),
             pltpu.VMEM((4 * cap, hidden), jnp.float32),
             dma((3,)),
@@ -309,7 +298,15 @@
             bytes_accessed=6 * width * hidden,
             transcendentals=rows * 4 * hidden,
         ),
-    )(tokens, routes, route_weights, w_gate, w_up, w_down)
+    )(tokens, routes.T, w_gate, w_up, w_down)
+    factor = jnp.sum(jnp.where(routes < n, route_weights, 0.0), axis=1)
+    picked = lax.dot_general(
+        selector,
+        returned.reshape(n * cap, width),
+        (((0,), (0,)), ((), ())),
+        preferred_element_type=jnp.float32,
+    )
+    return (factor[:, None] * picked).astype(bf16)
 
 
 def staged(tokens, routes, route_weights, w_gate, w_up, w_down):

time: 77.1 us -> 74.2 us (0.962)
  local copies, waits for them, and re-layouts: 4.91 us -> 0 us
  matrix products: 0 us -> 2.56 us
  Pallas kernels: 72 us -> 70.2 us
    unnamed x3 -> x0, local copies, waits for them, and re-layouts: 4.91 us -> none
    dot_general x0 -> x1, matrix products: none -> 2.56 us  [fused(): lax.dot_general(selector, returned.reshape(n * cap, width), (((0,), (0,))...]
    pallas_call x1, Pallas kernels: 72 us -> 70.2 us  [fused(): pl.pallas_call(functools.partial(layer_kernel, n, cap, tile), out_shape=(...]
where the time goes in v2:
time: 74.2 us; the launch traced here: 73.5 us
  Pallas kernels  70.2 us (95%)
  matrix products  2.56 us (3%)
    pallas_call x1, Pallas kernels, fused(): pl.pallas_call(functools.partial(layer_kernel, n, cap, tile), out_shape=(...  70.2 us
    dot_general x1, matrix products, fused(): lax.dot_general(selector, returned.reshape(n * cap, width), (((0,), (0,))...  2.56 us

profile of v2, /device:TPU:9, one launch (start us, length us, event | category | flops | bytes accessed | tf_op | source)
XLA Modules:
  0.0 73.5 jit_solution(8829483130787217552)
XLA Ops:
  0.0 0.7 select_reduce_fusion
  0.7 70.2 %shard_map.64 = (bf16[4,16,7168]{2,1,0:T(8,128)(2,1)}, bf16[64,64]{1,0:T(8,128)(2,1)}) custom-call(bf16[64,7168]{1,0:T(8,128)(2,1)} %tokens_ref.1, s32[8,64]{1,0:T(8,128)} %bitcast.5, bf16[1,7168,512]{2,1,0:T(8,128)(2,1)} %gate_hbm.1, bf16[1,7168,512]{2,1,0:T(8,128)(2,1)} %up_hbm.1, bf16[1,512,7168]{2,1,0:T(8,128)(2,1)} %down_hbm.1), custom_call_target="tpu_custom_call" | custom-call | flops 5637144576 | bytes 22020096 | tf_op jit(solution)/shard_map/pallas_call | solution.py:258
  70.9 2.6 %fusion = bf16[64,7168]{1,0:T(8,128)(2,1)} fusion(bf16[64,64]{1,0:T(8,128)(2,1)} %get-tuple-element.7, bf16[64,7168]{1,0:T(8,128)(2,1)} %bitcast.4, f32[64]{0:T(128)S(1)} %select_reduce_fusion), kind=kOutput, calls=%fused_computation.1 | convolution fusion | flops 59637760 | bytes 1843456 | tf_op jit(solution)/shard_map/dot_general | solution.py:303

commit v3 on v2

--- a/solution.py
+++ b/solution.py
@@ -8,8 +8,11 @@
 from jax.sharding import PartitionSpec as P
 
 MESH = pl.DeviceIdType.MESH
-ORDER = (0, 1, 2, 3)
-ISSUE = ((1, 2, 3), (), (), ())
+STEPS = (
+    *("Z1", "R0", "C0", "Z2", "R1", "C1", "S1"),
+    *("Z3", "R2", "C2", "X1", "S2", "R3", "C3"),
+    *("X2", "S3", "S0", "X3", "X0"),
+)
 
 
 def settle(values):
@@ -141,22 +144,17 @@
     def arrived(dst, send, recv):
         remote(dst, dst, send, recv, e, s_x).wait_recv()
 
-    def issue(ks):
-        for k in ks:
-            launch(
-                remote(
-                    outgoing.at[planes[k]],
-                    rows_in.at[e, s],
-                    dz_send.at[k],
-                    dz_recv.at[k],
-                    planes[k],
-                    s,
-                )
+    for k in range(1, n_major):
+        launch(
+            remote(
+                outgoing.at[planes[k]],
+                rows_in.at[e, s],
+                dz_send.at[k],
+                dz_recv.at[k],
+                planes[k],
+                s,
             )
-
-    order = ORDER if n_major == 4 else tuple(range(n_major))
-    plan = ISSUE if n_major == 4 else (order[1:],) + ((),) * (n_major - 1)
-    issue(plan[0])
+        )
     spread(0)
 
     def compute(k):
@@ -221,25 +219,27 @@
                 )
             )
 
-    for i, k in enumerate(order):
-        if i + 1 < n_major:
-            later = order[i + 1]
-            arrived(rows_in.at[planes[later], s], dz_send.at[later], dz_recv.at[later])
-            issue(plan[i + 1])
-            spread(later)
+    def bring(k):
+        arrived(rows_in.at[planes[k], s], dz_send.at[k], dz_recv.at[k])
+        spread(k)
+
+    def relay(k):
         far = rows_in.at[planes[k], s_x]
         arrived(far, dx_send.at[k], dx_recv.at[k])
         launch(remote(far, far, dc_send.at[k, 1], dc_recv.at[k, 1], e, s_core))
+
+    def work(k):
         arrived(rows_in.at[planes[k], s_core], dc_send.at[k, 0], dc_recv.at[k, 0])
         arrived(rows_in.at[planes[k], s_far], dc_send.at[k, 1], dc_recv.at[k, 1])
         compute(k)
-        if i >= 1:
-            x_sum(order[i - 1])
-        core_sum(k)
-    x_sum(order[-1])
-
-    for k in order[1:]:
+
+    does = {"Z": bring, "R": relay, "C": work, "S": core_sum, "X": x_sum}
+    for step in STEPS:
+        does[step[0]](int(step[1]))
+
+    for k in range(1, n_major):
         arrived(returned.at[planes[k]], rz_send.at[k], rz_recv.at[k])
+
     for copy in sent:
         copy.wait_send()
 
@@ -354,7 +354,7 @@
     n_major = lax.axis_size("ep")
     rows = args[0].shape[0]
     whole_tiles = rows % n_major == 0 and (rows // n_major) % 16 == 0
-    if whole_tiles and lax.axis_size("sub") == 4 and n_major & (n_major - 1) == 0:
+    if whole_tiles and lax.axis_size("sub") == 4 and n_major == 4:
         return fused(*args)
     return staged(*args)
 

time: 74.2 us -> 73.2 us (0.987)
  Pallas kernels: 70.2 us -> 68.7 us
    pallas_call x1, Pallas kernels: 70.2 us -> 68.7 us  [fused(): pl.pallas_call(functools.partial(layer_kernel, n, cap, tile), out_shape=(...]
where the time goes in v3:
time: 73.2 us; the launch traced here: 71.9 us
  Pallas kernels  68.7 us (94%)
  matrix products  2.56 us (3%)
    pallas_call x1, Pallas kernels, fused(): pl.pallas_call(functools.partial(layer_kernel, n, cap, tile), out_shape=(...  68.7 us
    dot_general x1, matrix products, fused(): lax.dot_general(selector, returned.reshape(n * cap, width), (((0,), (0,))...  2.56 us

profile of v3, /device:TPU:9, one launch (start us, length us, event | category | flops | bytes accessed | tf_op | source)
XLA Modules:
  0.0 71.9 jit_solution(11494179571292068666)
XLA Ops:
  0.0 0.7 %select_reduce_fusion = f32[64]{0:T(128)S(1)} fusion(f32[64,8]{0,1:T(8,128)} %param.8, s32[64,8]{0,1:T(8,128)} %param.7), kind=kLoop, calls=%fused_computation.2 | loop fusion | flops 1472 | bytes 4352 | tf_op jit(solution)/shard_map/reduce_sum | solution.py:302
  0.7 68.7 %shard_map.64 = (bf16[4,16,7168]{2,1,0:T(8,128)(2,1)}, bf16[64,64]{1,0:T(8,128)(2,1)}) custom-call(bf16[64,7168]{1,0:T(8,128)(2,1)} %tokens_ref.1, s32[8,64]{1,0:T(8,128)} %bitcast.5, bf16[1,7168,512]{2,1,0:T(8,128)(2,1)} %gate_hbm.1, bf16[1,7168,512]{2,1,0:T(8,128)(2,1)} %up_hbm.1, bf16[1,512,7168]{2,1,0:T(8,128)(2,1)} %down_hbm.1), custom_call_target="tpu_custom_call" | custom-call | flops 5637144576 | bytes 22020096 | tf_op jit(solution)/shard_map/pallas_call | solution.py:258
  69.4 2.6 %fusion = bf16[64,7168]{1,0:T(8,128)(2,1)} fusion(bf16[64,64]{1,0:T(8,128)(2,1)} %get-tuple-element.7, bf16[64,7168]{1,0:T(8,128)(2,1)} %bitcast.4, f32[64]{0:T(128)S(1)} %select_reduce_fusion), kind=kOutput, calls=%fused_computation.1 | convolution fusion | flops 59637760 | bytes 1843456 | tf_op jit(solution)/shard_map/dot_general | solution.py:303

commit v4 on v3

--- a/solution.py
+++ b/solution.py
@@ -144,6 +144,7 @@
     def arrived(dst, send, recv):
         remote(dst, dst, send, recv, e, s_x).wait_recv()
 
+    spread(0)
     for k in range(1, n_major):
         launch(
             remote(
@@ -155,7 +156,6 @@
                 s,
             )
         )
-    spread(0)
 
     def compute(k):
         plane = planes[k]

time: 73.2 us -> 73.3 us (level)
  no operation moved by 1% of the time
where the time goes in v4:
time: 73.3 us; the launch traced here: 71.9 us
  Pallas kernels  68.6 us (94%)
  matrix products  2.56 us (3%)
    pallas_call x1, Pallas kernels, fused(): pl.pallas_call(functools.partial(layer_kernel, n, cap, tile), out_shape=(...  68.6 us
    dot_general x1, matrix products, fused(): lax.dot_general(selector, returned.reshape(n * cap, width), (((0,), (0,))...  2.56 us

profile of v4, /device:TPU:9, one launch (start us, length us, event | category | flops | bytes accessed | tf_op | source)
XLA Modules:
  0.0 71.9 jit_solution(7864592875934196883)
XLA Ops:
  0.0 0.7 %select_reduce_fusion = f32[64]{0:T(128)S(1)} fusion(f32[64,8]{0,1:T(8,128)} %param.8, s32[64,8]{0,1:T(8,128)} %param.7), kind=kLoop, calls=%fused_computation.2 | loop fusion | flops 1472 | bytes 4352 | tf_op jit(solution)/shard_map/reduce_sum | solution.py:302
  0.7 68.6 %shard_map.64 = (bf16[4,16,7168]{2,1,0:T(8,128)(2,1)}, bf16[64,64]{1,0:T(8,128)(2,1)}) custom-call(bf16[64,7168]{1,0:T(8,128)(2,1)} %tokens_ref.1, s32[8,64]{1,0:T(8,128)} %bitcast.5, bf16[1,7168,512]{2,1,0:T(8,128)(2,1)} %gate_hbm.1, bf16[1,7168,512]{2,1,0:T(8,128)(2,1)} %up_hbm.1, bf16[1,512,7168]{2,1,0:T(8,128)(2,1)} %down_hbm.1), custom_call_target="tpu_custom_call" | custom-call | flops 5637144576 | bytes 22020096 | tf_op jit(solution)/shard_map/pallas_call | solution.py:258
  69.4 2.6 %fusion = bf16[64,7168]{1,0:T(8,128)(2,1)} fusion(bf16[64,64]{1,0:T(8,128)(2,1)} %get-tuple-element.7, bf16[64,7168]{1,0:T(8,128)(2,1)} %bitcast.4, f32[64]{0:T(128)S(1)} %select_reduce_fusion), kind=kOutput, calls=%fused_computation.1 | convolution fusion | flops 59637760 | bytes 1843456 | tf_op jit(solution)/shard_map/dot_general | solution.py:303
